TPU v7x, 512 devices: a whole 4x4x16 slice. The times are simulated.
512 devices in a mesh: seq: 128 (over x, y, z_hi, core), user: 4 (over z_lo).
Axes of the slice: x: 4, y: 4, z: 16 (z_hi: 4, z_lo: 4; z = z_hi * 4 + z_lo), core: 2. Of those that a mesh axis runs over, the one named last changes fastest.
Arguments:
- inputs: bfloat16 [4, 131072, 256], P('user', 'seq'), may hold values from -6 to 6
- kernel_weight_first: bfloat16 [3, 256, 256], replicated, may hold values from -0.21875 to 0.21875
- norm_gain_first: float32 [256], replicated, may hold values from 0.1 to 1.9
- norm_bias_first: float32 [256], replicated, may hold values from -0.5 to 0.5
- kernel_weight_second: bfloat16 [3, 256, 256], replicated, may hold values from -0.21875 to 0.21875
- norm_gain_second: float32 [256], replicated, may hold values from 0.1 to 1.9
- norm_bias_second: float32 [256], replicated, may hold values from -0.5 to 0.5
- cotangent: bfloat16 [4, 131072, 256], P('user', 'seq'), may hold values from -9 to 9
Outputs:
- grad_inputs: bfloat16 [4, 131072, 256], P('user', 'seq')
- grad_weight_one: float32 [3, 256, 256], replicated
- grad_gain_one: float32 [256], replicated
- grad_bias_one: float32 [256], replicated
- grad_weight_two: float32 [3, 256, 256], replicated
- grad_gain_two: float32 [256], replicated
- grad_bias_two: float32 [256], replicated
All inputs are finite; a program needn't handle non-finite values.
Results may differ from a plain program's by a relative error of at most 0.012.
Values may be sent and summed in bfloat16 or wider, within the bound.
A program may use at most 64 MiB of HBM per device.

v0:
```python
import jax
import jax.numpy as jnp
from jax import lax
from jax.sharding import PartitionSpec as P

DILATION_FIRST1 = 1024
DILATION_SECOND2 = 2048


EPSILON = 1e-05


def passed_along(shard, axis, by):
    size = lax.axis_size(axis)
    pairs = [(i, i + by) for i in range(size) if 0 <= i + by < size]
    return lax.ppermute(shard, axis, pairs)


def activate(values):
    return values * jax.nn.sigmoid(values)


def activate_slope(values):
    sigma = jax.nn.sigmoid(values)
    return sigma * (1.0 + values * (1.0 - sigma))


def past_taps(blocks, stride):
    tap_near = passed_along(blocks, "seq", stride)
    tap_far = passed_along(blocks, "seq", 2 * stride)
    return (tap_near, tap_far)


def future_taps(blocks, stride):
    tap_near = passed_along(blocks, "seq", -stride)
    tap_far = passed_along(blocks, "seq", -2 * stride)
    return (tap_near, tap_far)


def normalize(pre):
    center = jnp.mean(pre, axis=-1, keepdims=True)
    spread = jnp.mean(jnp.square(pre - center), axis=-1, keepdims=True)
    inverse = lax.rsqrt(spread + EPSILON)
    return ((pre - center) * inverse, inverse)


def residual_layer_forward(blocks, weight, gain, bias, stride, past_rule):
    channels = blocks.shape[-1]
    shifted = (blocks,) + past_rule(blocks, stride)
    flat_taps = [piece.reshape(-1, channels) for piece in shifted]
    pre = jnp.dot(flat_taps[0], weight[0], preferred_element_type=jnp.float32)
    for offset in range(1, 3):
        pre = pre + jnp.dot(flat_taps[offset], weight[offset], preferred_element_type=jnp.float32)
    normed, inverse = normalize(pre)
    active = normed * gain + bias
    return (flat_taps, normed, inverse, active)


def residual_layer_backward(
    g_out, flat_taps, normed, inverse, active, weight, gain, stride, shape, future_rule
):
    g_act = g_out * activate_slope(active)
    gain_sum = jnp.sum(g_act * normed, axis=0)
    bias_sum = jnp.sum(g_act, axis=0)
    g_norm = g_act * gain
    g_pre = inverse * (
        g_norm
        - jnp.mean(g_norm, axis=-1, keepdims=True)
        - normed * jnp.mean(g_norm * normed, axis=-1, keepdims=True)
    )
    g_pre = g_pre.astype(jnp.bfloat16)
    weight_sum = jnp.stack(
        [
            lax.dot_general(
                piece, g_pre, (((0,), (0,)), ((), ())), preferred_element_type=jnp.float32
            )
            for piece in flat_taps
        ]
    )
    fut_near, fut_far = future_rule(g_pre.reshape(shape), stride)
    moved_all = (g_pre, fut_near.reshape(g_pre.shape), fut_far.reshape(g_pre.shape))
    g_in = g_out
    for offset in range(3):
        g_in = g_in + lax.dot_general(
            moved_all[offset],
            weight[offset],
            (((1,), (1,)), ((), ())),
            preferred_element_type=jnp.float32,
        )
    return (g_in.astype(jnp.bfloat16), weight_sum, gain_sum, bias_sum)


def shards(
    inputs,
    kernel_weight_first,
    norm_gain_first,
    norm_bias_first,
    kernel_weight_second,
    norm_gain_second,
    norm_bias_second,
    cotangent,
):
    members, history_length, channels = inputs.shape
    shape = inputs.shape
    grad_scale = 1.0 / jnp.sqrt(
        jnp.float32(members * lax.axis_size("user") * history_length * lax.axis_size("seq"))
    )
    tap_stride_first = DILATION_FIRST1 // history_length
    tap_stride_second = DILATION_SECOND2 // history_length
    work_in, work_ct = (inputs, cotangent)
    work_shape = work_in.shape
    taps_one, normalized_first, inverse_deviation_first, activation_first = residual_layer_forward(
        work_in, kernel_weight_first, norm_gain_first, norm_bias_first, tap_stride_first, past_taps
    )
    hidden_state = (
        work_in.reshape(-1, channels).astype(jnp.float32) + activate(activation_first)
    ).astype(jnp.bfloat16)
    taps_two, normalized_second, inverse_deviation_second, activation_second = (
        residual_layer_forward(
            hidden_state.reshape(work_shape),
            kernel_weight_second,
            norm_gain_second,
            norm_bias_second,
            tap_stride_second,
            past_taps,
        )
    )
    g_top = work_ct.reshape(-1, channels).astype(jnp.float32)
    gradient_hidden, weight_total_second, gain_total_second, bias_total_second = (
        residual_layer_backward(
            g_top,
            taps_two,
            normalized_second,
            inverse_deviation_second,
            activation_second,
            kernel_weight_second,
            norm_gain_second,
            tap_stride_second,
            work_shape,
            future_taps,
        )
    )
    gradient_input_rows, weight_total_first, gain_total_first, bias_total_first = (
        residual_layer_backward(
            gradient_hidden.astype(jnp.float32),
            taps_one,
            normalized_first,
            inverse_deviation_first,
            activation_first,
            kernel_weight_first,
            norm_gain_first,
            tap_stride_first,
            work_shape,
            future_taps,
        )
    )
    summed = lax.psum(
        (
            weight_total_first,
            gain_total_first,
            bias_total_first,
            weight_total_second,
            gain_total_second,
            bias_total_second,
        ),
        ("seq", "user"),
    )
    (
        weight_total_first,
        gain_total_first,
        bias_total_first,
        weight_total_second,
        gain_total_second,
        bias_total_second,
    ) = summed
    grad_out = gradient_input_rows.reshape(shape)
    return (
        grad_out,
        weight_total_first * grad_scale,
        gain_total_first * grad_scale,
        bias_total_first * grad_scale,
        weight_total_second * grad_scale,
        gain_total_second * grad_scale,
        bias_total_second * grad_scale,
    )


def solution(mesh):
    placed = (P("user", "seq", None), P(), P(), P(), P(), P(), P(), P("user", "seq", None))
    return jax.shard_map(
        shards,
        mesh=mesh,
        in_specs=placed,
        out_specs=(P("user", "seq", None), P(), P(), P(), P(), P(), P()),
        check_vma=False,
    )
```

profile of v0, /device:TPU:1, one launch (start us, length us, event | category | flops | bytes accessed | tf_op | source)
XLA Modules:
  0.0 915.7 jit_solution(5203911485155496763)
XLA Ops:
  7.2 10.3 %collective-permute-start = (bf16[1,1024,256]{2,1,0:T(8,128)(2,1)}, bf16[1,1024,256]{2,1,0:T(8,128)(2,1)S(1)}, u32[]{:S(2)}, u32[]{:S(2)}) collective-permute-start(bf16[1,1024,256]{2,1,0:T(8,128)(2,1)} %param.8), channel_id=1, source_target_pairs={{0,4},{4,8},{8,12},{12,16},{16,20},{20,24},{24,28},{28,32},{32,36}... | collective-permute-start | bytes 1572872 | tf_op jit(solution)/shard_map/ppermute | solution.py:16
  17.6 9.6 %collective-permute-start.1 = (bf16[1,1024,256]{2,1,0:T(8,128)(2,1)}, bf16[1,1024,256]{2,1,0:T(8,128)(2,1)}, u32[]{:S(2)}, u32[]{:S(2)}) collective-permute-start(bf16[1,1024,256]{2,1,0:T(8,128)(2,1)} %param.8), channel_id=1, source_target_pairs={{0,8},{4,12},{8,16},{12,20},{16,24},{20,28},{24,32},{28,36},{32,40... | collective-permute-start | bytes 1572872 | tf_op jit(solution)/shard_map/ppermute | solution.py:16
  27.2 1.2 copy.16
  28.8 5.7 collective-permute-done
  35.3 13.0 %collective-permute-done.1 = bf16[1,1024,256]{2,1,0:T(8,128)(2,1)} collective-permute-done((bf16[1,1024,256]{2,1,0:T(8,128)(2,1)}, bf16[1,1024,256]{2,1,0:T(8,128)(2,1)}, u32[]{:S(2)}, u32[]{:S(2)}) %collective-permute-start.1) | collective-permute-done | bytes 524320 | tf_op jit(solution)/shard_map/ppermute | solution.py:16
  48.3 1.4 fusion.47
  51.0 48.0 %collective-permute-start.2 = (bf16[1,1024,256]{1,2,0:T(8,128)(2,1)S(1)}, bf16[1,1024,256]{1,2,0:T(8,128)(2,1)S(1)}, u32[]{:S(2)}, u32[]{:S(2)}) collective-permute-start(bf16[1,1024,256]{1,2,0:T(8,128)(2,1)S(1)} %bitcast.124), channel_id=1, source_target_pairs={{0,8},{4,12},{8,16},{12,20},{16,24},{20,28},{24,32},{28,36},{32,40... | collective-permute-start | bytes 1572872 | tf_op jit(solution)/shard_map/ppermute | solution.py:16
  99.0 1.2 copy.15
  100.2 7.8 collective-permute-start.3
  108.0 1.2 fusion.27
  109.6 19.5 %collective-permute-done.3 = bf16[1,1024,256]{1,2,0:T(8,128)(2,1)S(1)} collective-permute-done((bf16[1,1024,256]{1,2,0:T(8,128)(2,1)S(1)}, bf16[1,1024,256]{1,2,0:T(8,128)(2,1)S(1)}, u32[]{:S(2)}, u32[]{:S(2)}) %collective-permute-start.3) | collective-permute-done | bytes 524320 | tf_op jit(solution)/shard_map/ppermute | solution.py:16
  130.4 1.5 multiply_reduce_fusion
  132.5 1.3 collective-permute-start.5
  133.8 1.3 collective-permute-start.4
  137.1 65.1 %collective-permute-done.5 = bf16[1,1024,256]{1,2,0:T(8,128)(2,1)S(1)} collective-permute-done((bf16[1,1024,256]{1,2,0:T(8,128)(2,1)S(1)}, bf16[1,1024,256]{1,2,0:T(8,128)(2,1)S(1)}, u32[]{:S(2)}, u32[]{:S(2)}) %collective-permute-start.5) | collective-permute-done | bytes 524320 | tf_op jit(solution)/shard_map/ppermute | solution.py:16
  202.5 1.6 multiply_reduce_fusion.1
  204.8 1.3 collective-permute-start.7
  206.1 1.9 collective-permute-start.6
  208.7 230.2 %all-reduce = (f32[256]{0:T(256)S(1)}, f32[256]{0:T(256)S(1)}, f32[256]{0:T(256)S(1)}, f32[256]{0:T(256)S(1)}) all-reduce(f32[256]{0:T(256)S(1)} %copy-done.12, f32[256]{0:T(256)S(1)} %copy-done.13, f32[256]{0:T(256)S(1)} %get-tuple-element.14, f32[256]{0:T(256)S(1)} %copy-done.8), channel_id=1, replica_groups=mesh['seq'=128,'user'=4] {'seq','user'}, use_global_device_ids=true, to_apply=%region_10.0 | all-reduce | flops 1024 | bytes 8192 | tf_op jit(solution)/shard_map/psum | solution.py:157
  440.5 1.4 convolution_bitcast_fusion.3
  445.7 459.5 %all-reduce.4.cloned.1.call-done = (f32[3,256,256]{1,2,0:T(8,128)}, f32[3,256,256]{1,2,0:T(8,128)}) async-done(((f32[3,256,256]{1,2,0:T(8,128)}, f32[3,256,256]{1,2,0:T(8,128)}), (f32[3,256,256]{1,2,0:T(8,128)}, f32[3,256,256]{1,2,0:T(8,128)})) %all-reduce.4.cloned.1.call-update) | async-done | bytes 1572880 | tf_op jit(solution)/shard_map/psum | solution.py:157
  905.2 1.2 broadcast_multiply_fusion.1
  906.5 1.1 copy.27
  907.7 1.1 copy.28
  (68 shorter events, 13.6 us)
Async XLA Ops:
  7.2 21.3 %copy-start = (bf16[1,1024,256]{2,1,0:T(8,128)(2,1)S(1)}, bf16[1,1024,256]{2,1,0:T(8,128)(2,1)}, u32[]{:S(2)}) copy-start(bf16[1,1024,256]{2,1,0:T(8,128)(2,1)} %param.8) | copy-start | bytes 1572868
  7.2 21.3 %copy-start.3 = (bf16[3,256,256]{2,1,0:T(8,128)(2,1)S(1)}, bf16[3,256,256]{2,1,0:T(8,128)(2,1)}, u32[]{:S(2)}) copy-start(bf16[3,256,256]{2,1,0:T(8,128)(2,1)} %param.9) | copy-start | bytes 1179652
  7.2 898.0 %all-reduce.4.cloned.1.call-start = ((), (), s32[]{:S(2)}) async-start(), calls=%async_computation | async-start | bytes 3145728 | tf_op jit(solution)/shard_map/psum | solution.py:157
  7.2 27.2 %collective-permute-start = (bf16[1,1024,256]{2,1,0:T(8,128)(2,1)}, bf16[1,1024,256]{2,1,0:T(8,128)(2,1)S(1)}, u32[]{:S(2)}, u32[]{:S(2)}) collective-permute-start(bf16[1,1024,256]{2,1,0:T(8,128)(2,1)} %param.8), channel_id=1, source_target_pairs={{0,4},{4,8},{8,12},{12,16},{16,20},{20,24},{24,28},{28,32},{32,36}... | collective-permute-start | bytes 1572872 | tf_op jit(solution)/shard_map/ppermute | solution.py:16
  17.6 30.7 %collective-permute-start.1 = (bf16[1,1024,256]{2,1,0:T(8,128)(2,1)}, bf16[1,1024,256]{2,1,0:T(8,128)(2,1)}, u32[]{:S(2)}, u32[]{:S(2)}) collective-permute-start(bf16[1,1024,256]{2,1,0:T(8,128)(2,1)} %param.8), channel_id=1, source_target_pairs={{0,8},{4,12},{8,16},{12,20},{16,24},{20,28},{24,32},{28,36},{32,40... | collective-permute-start | bytes 1572872 | tf_op jit(solution)/shard_map/ppermute | solution.py:16
  34.5 0.8 copy-start.1
  49.8 0.7 copy-start.7
  49.8 0.7 copy-start.10
  51.0 58.3 %collective-permute-start.2 = (bf16[1,1024,256]{1,2,0:T(8,128)(2,1)S(1)}, bf16[1,1024,256]{1,2,0:T(8,128)(2,1)S(1)}, u32[]{:S(2)}, u32[]{:S(2)}) collective-permute-start(bf16[1,1024,256]{1,2,0:T(8,128)(2,1)S(1)} %bitcast.124), channel_id=1, source_target_pairs={{0,8},{4,12},{8,16},{12,20},{16,24},{20,28},{24,32},{28,36},{32,40... | collective-permute-start | bytes 1572872 | tf_op jit(solution)/shard_map/ppermute | solution.py:16
  100.2 9.0 copy-start.4
  100.2 28.9 %collective-permute-start.3 = (bf16[1,1024,256]{1,2,0:T(8,128)(2,1)S(1)}, bf16[1,1024,256]{1,2,0:T(8,128)(2,1)S(1)}, u32[]{:S(2)}, u32[]{:S(2)}) collective-permute-start(bf16[1,1024,256]{1,2,0:T(8,128)(2,1)S(1)} %bitcast.125), channel_id=1, source_target_pairs={{0,16},{4,20},{8,24},{12,28},{16,32},{20,36},{24,40},{28,44},{32,4... | collective-permute-start | bytes 1572872 | tf_op jit(solution)/shard_map/ppermute | solution.py:16
  129.7 0.7 copy-start.6
  129.7 0.7 copy-start.9
  132.5 69.6 %collective-permute-start.5 = (bf16[1,1024,256]{1,2,0:T(8,128)(2,1)S(1)}, bf16[1,1024,256]{1,2,0:T(8,128)(2,1)S(1)}, u32[]{:S(2)}, u32[]{:S(2)}) collective-permute-start(bf16[1,1024,256]{1,2,0:T(8,128)(2,1)S(1)} %bitcast.122), channel_id=1, source_target_pairs={{16,0},{20,4},{24,8},{28,12},{32,16},{36,20},{40,24},{44,28},{48,3... | collective-permute-start | bytes 1572872 | tf_op jit(solution)/shard_map/ppermute | solution.py:16
  133.8 68.6 %collective-permute-start.4 = (bf16[1,1024,256]{1,2,0:T(8,128)(2,1)S(1)}, bf16[1,1024,256]{1,2,0:T(8,128)(2,1)S(1)}, u32[]{:S(2)}, u32[]{:S(2)}) collective-permute-start(bf16[1,1024,256]{1,2,0:T(8,128)(2,1)S(1)} %bitcast.123), channel_id=1, source_target_pairs={{8,0},{12,4},{16,8},{20,12},{24,16},{28,20},{32,24},{36,28},{40,32... | collective-permute-start | bytes 1572872 | tf_op jit(solution)/shard_map/ppermute | solution.py:16
  137.1 65.4 %copy-start.11 = (f32[256]{0:T(256)S(1)}, f32[256]{0:T(256)}, u32[]{:S(2)}) copy-start(f32[256]{0:T(256)} %param.11) | copy-start | bytes 3076
  204.4 3.6 copy-start.12
  204.4 3.6 copy-start.13
  204.8 239.3 %collective-permute-start.7 = (bf16[1,1024,256]{1,2,0:T(8,128)(2,1)S(1)}, bf16[1,1024,256]{1,2,0:T(8,128)(2,1)S(1)}, u32[]{:S(2)}, u32[]{:S(2)}) collective-permute-start(bf16[1,1024,256]{1,2,0:T(8,128)(2,1)S(1)} %bitcast.120), channel_id=1, source_target_pairs={{8,0},{12,4},{16,8},{20,12},{24,16},{28,20},{32,24},{36,28},{40,32... | collective-permute-start | bytes 1572872 | tf_op jit(solution)/shard_map/ppermute | solution.py:16
  206.1 238.3 %collective-permute-start.6 = (bf16[1,1024,256]{1,2,0:T(8,128)(2,1)S(1)}, bf16[1,1024,256]{1,2,0:T(8,128)(2,1)S(1)}, u32[]{:S(2)}, u32[]{:S(2)}) collective-permute-start(bf16[1,1024,256]{1,2,0:T(8,128)(2,1)S(1)} %bitcast.121), channel_id=1, source_target_pairs={{4,0},{8,4},{12,8},{16,12},{20,16},{24,20},{28,24},{32,28},{36,32}... | collective-permute-start | bytes 1572872 | tf_op jit(solution)/shard_map/ppermute | solution.py:16
  208.0 0.7 copy-start.8
  440.5 1.4 copy-start.2
  906.5 1.2 copy-start.5
Sparse Core Ops, SparseCore 0:
  443.3 461.8 all-reduce.3
where the time goes:
time: 917 us; the launch traced here: 916 us
  waiting for transfers between devices  563 us (61%)
  blocking collectives  230 us (25%)
  starting transfers between devices  81.5 us (9%)
  between operations  14.5 us (2%)
  matrix products  10.2 us (1%)
    psum x1, waiting for transfers between devices, shards(): lax.psum((weight_total_first, gain_total_first, bias_total_first, weight_...  460 us
    psum x1, blocking collectives, shards(): lax.psum((weight_total_first, gain_total_first, bias_total_first, weight_...  230 us
    ppermute x8, waiting for transfers between devices, passed_along(): return lax.ppermute(shard, axis, pairs)  103 us
    ppermute x8, starting transfers between devices, passed_along(): return lax.ppermute(shard, axis, pairs)  81.5 us
  transfers between devices with their start and end apart: 9, of which 5 were waited for; matrix products, arithmetic and copies ran while one was open for 2% of the time, Pallas kernels for 0%

commit v1 on v0

v1 whole, which is shorter than its diff:
```python
import functools

import jax
import jax.numpy as jnp
from jax import lax
from jax.experimental import pallas as pl
from jax.experimental.pallas import tpu as pltpu
from jax.sharding import PartitionSpec as P

DILATION_FIRST1 = 1024
DILATION_SECOND2 = 2048
EPSILON = 1e-05
GROUP = 8
MESH = pl.DeviceIdType.MESH
F32 = jnp.float32
BF16 = jnp.bfloat16


def dot(a, b):
    return jnp.dot(a, b, preferred_element_type=F32)


def mean_c(values):
    return jnp.mean(values, axis=-1, keepdims=True)


def kernel(
    M, G, U, R, scale,
    x_ref, ct_ref, w1_ref, w2_ref, gain1, bias1, gain2, bias2,
    out_ref, dw_ref, dg1, db1, dg2, db2,
    xe, cte, he, g2e, g1e, xt, ht, w1, w2, w1t, w2t,
    n1, i1, s1, n2, i2, s2, gh, ov,
    part, core_in, shard, r1, r2, r3, final,
    loc_sem, xs, xr, cs, cr, os_, or_, hs, hr, ps, pr, gs, gr, us, ur, zs, zr, as_, ar, bs, br,
):
    C = x_ref.shape[1]
    NT = M // 2
    T = 2 * R
    KC = 3 * C
    SH = KC // G
    s, u = lax.axis_index("seq"), lax.axis_index("user")
    g, m = s // M, s % M
    core = m % 2
    z = m // 2

    def member(p):
        return {"seq": g * M + p, "user": u}

    def group(p):
        return {"seq": p * M + m, "user": u}

    def user(p):
        return {"seq": s, "user": p}

    def remote(src, dst, ss, rs, device):
        return pltpu.make_async_remote_copy(
            src_ref=src, dst_ref=dst, send_sem=ss, recv_sem=rs, device_id=device, device_id_type=MESH
        )

    def rows(start, size):
        return pl.ds(pl.multiple_of(start, R), size)

    barrier = pltpu.get_barrier_semaphore()
    for j in range(1, M):
        pl.semaphore_signal(barrier, inc=1, device_id=member((m + j) % M), device_id_type=MESH)
    for j in range(1, G):
        pl.semaphore_signal(barrier, inc=1, device_id=group((g + j) % G), device_id_type=MESH)
    for j in range(1, U):
        pl.semaphore_signal(barrier, inc=1, device_id=user((u + j) % U), device_id_type=MESH)

    own = rows(m * R, R)
    local = [
        pltpu.make_async_copy(w1_ref, w1, loc_sem.at[0]),
        pltpu.make_async_copy(w2_ref, w2, loc_sem.at[1]),
        pltpu.make_async_copy(x_ref.at[own], xe.at[rows((2 + m) * R, R)], loc_sem.at[2]),
        pltpu.make_async_copy(ct_ref.at[own], cte.at[rows(m * R, R)], loc_sem.at[3]),
    ]
    for copy in local:
        copy.start()

    pl.semaphore_wait(barrier, M + G + U - 3)

    order = [M // 2, M // 2 + 1] + [j for j in range(M - 1, 0, -1) if j not in (M // 2, M // 2 + 1)]

    def x_copy(j):
        p = (m + j) % M
        return remote(x_ref.at[rows(p * R, R)], xe.at[rows((2 + m) * R, R)], xs.at[j], xr.at[j], member(p))

    def ct_copy(j):
        p = (m + j) % M
        return remote(ct_ref.at[rows(p * R, R)], cte.at[rows(m * R, R)], cs.at[j], cr.at[j], member(p))

    for j in order:
        x_copy(j).start()

    @pl.when(g == 0)
    def _():
        xe[0 : 2 * R] = jnp.zeros((2 * R, C), BF16)
        he[0 : 4 * R] = jnp.zeros((4 * R, C), BF16)

    @pl.when(g == G - 1)
    def _():
        g2e[M * R : (M + 4) * R] = jnp.zeros((4 * R, C), BF16)
        g1e[M * R : (M + 2) * R] = jnp.zeros((2 * R, C), BF16)

    later, earlier = group((g + 1) % G), group((g + G - 1) % G)
    x_halo = remote(xe.at[M * R : (M + 2) * R], xe.at[0 : 2 * R], hs.at[0], hr.at[0], later)
    h_halo = remote(he.at[M * R : (M + 4) * R], he.at[0 : 4 * R], hs.at[1], hr.at[1], later)
    g2_halo = remote(g2e.at[0 : 4 * R], g2e.at[M * R : (M + 4) * R], hs.at[2], hr.at[2], earlier)
    g1_halo = remote(g1e.at[0 : 2 * R], g1e.at[M * R : (M + 2) * R], hs.at[3], hr.at[3], earlier)

    def start_if(cond, copy):
        @pl.when(cond)
        def _():
            copy.start()

    def recv_if(cond, copy):
        @pl.when(cond)
        def _():
            copy.wait_recv()

    def send_done_if(cond, copy):
        @pl.when(cond)
        def _():
            copy.wait_send()

    for copy in local:
        copy.wait()
    for k in range(3):
        w1t[k] = w1[k].T
        w2t[k] = w2[k].T

    for j in range(1, M):
        x_copy(j).wait()
    start_if(g < G - 1, x_halo)
    for j in order:
        ct_copy(j).start()

    ga1, be1, ga2, be2 = gain1[...], bias1[...], gain2[...], bias2[...]

    def layer_one(n, _):
        i = NT - 1 - n
        at = i * T
        recv_if((i == 0) & (g > 0), x_halo)
        here = xe[rows(at + 2 * R, T)]
        pre = dot(here, w1[0]) + dot(xe[rows(at + R, T)], w1[1]) + dot(xe[rows(at, T)], w1[2])
        away = pre - mean_c(pre)
        inverse = lax.rsqrt(mean_c(away * away) + EPSILON)
        normed = away * inverse
        active = normed * ga1 + be1
        sigma = 0.5 * jnp.tanh(0.5 * active) + 0.5
        he[rows(at + 4 * R, T)] = (here.astype(F32) + active * sigma).astype(BF16)
        mine = rows(at, T)
        n1[mine] = normed
        i1[mine] = jnp.broadcast_to(inverse, (T, 128))
        s1[mine] = sigma * (1.0 + active * (1.0 - sigma))
        start_if((i == NT - 2) & (g < G - 1), h_halo)
        return 0

    lax.fori_loop(0, NT, layer_one, 0)

    def layer_two(n, _):
        i = NT - 1 - n
        at = i * T
        recv_if((i == 1) & (g > 0), h_halo)
        pre = (
            dot(he[rows(at + 4 * R, T)], w2[0])
            + dot(he[rows(at + 2 * R, T)], w2[1])
            + dot(he[rows(at, T)], w2[2])
        )
        away = pre - mean_c(pre)
        inverse = lax.rsqrt(mean_c(away * away) + EPSILON)
        normed = away * inverse
        active = normed * ga2 + be2
        sigma = 0.5 * jnp.tanh(0.5 * active) + 0.5
        mine = rows(at, T)
        n2[mine] = normed
        i2[mine] = jnp.broadcast_to(inverse, (T, 128))
        s2[mine] = sigma * (1.0 + active * (1.0 - sigma))
        return 0

    lax.fori_loop(0, NT, layer_two, 0)

    def turn_h(i, _):
        ht[:, pl.ds(pl.multiple_of(i * T, 128), T)] = he[rows(i * T, T)].T
        return 0

    def turn_x(i, _):
        xt[:, pl.ds(pl.multiple_of(i * T, 128), T)] = xe[rows(i * T, T)].T
        return 0

    lax.fori_loop(0, NT + 2, turn_h, 0)
    lax.fori_loop(0, NT + 1, turn_x, 0)

    for j in range(1, M):
        ct_copy(j).wait()

    def norm_backward(grad, slope, normed, inverse, gain):
        g_act = grad * slope
        weighted = g_act * normed
        sums = (jnp.sum(weighted, axis=0, keepdims=True), jnp.sum(g_act, axis=0, keepdims=True))
        g_norm = g_act * gain
        g_pre = inverse * (g_norm - mean_c(g_norm) - normed * mean_c(weighted * gain))
        return g_pre.astype(BF16), sums

    zero = jnp.zeros((1, C), F32)

    def back_two(i, sums):
        mine = rows(i * T, T)
        g_pre, more = norm_backward(cte[mine].astype(F32), s2[mine], n2[mine], i2[mine][:, 0:1], ga2)
        g2e[mine] = g_pre
        start_if((i == 1) & (g > 0), g2_halo)
        return (sums[0] + more[0], sums[1] + more[1])

    gain_sum_two, bias_sum_two = lax.fori_loop(0, NT, back_two, (zero, zero))

    for k in range(3):
        part[1, k * C : (k + 1) * C] = dot(ht[:, (4 - 2 * k) * R : (4 - 2 * k + M) * R], g2e[0 : M * R])

    def back_one(i, sums):
        at = i * T
        recv_if((i == NT - 2) & (g < G - 1), g2_halo)
        mine = rows(at, T)
        total = (
            cte[mine].astype(F32)
            + dot(g2e[mine], w2t[0])
            + dot(g2e[rows(at + 2 * R, T)], w2t[1])
            + dot(g2e[rows(at + 4 * R, T)], w2t[2])
        )
        g_hidden = total.astype(BF16)
        gh[mine] = g_hidden
        g_pre, more = norm_backward(g_hidden.astype(F32), s1[mine], n1[mine], i1[mine][:, 0:1], ga1)
        g1e[mine] = g_pre
        start_if((i == 0) & (g > 0), g1_halo)
        return (sums[0] + more[0], sums[1] + more[1])

    gain_sum_one, bias_sum_one = lax.fori_loop(0, NT, back_one, (zero, zero))

    for k in range(3):
        part[0, k * C : (k + 1) * C] = dot(xt[:, (2 - k) * R : (2 - k + M) * R], g1e[0 : M * R])
    small = jnp.concatenate(
        [gain_sum_one, bias_sum_one, gain_sum_two, bias_sum_two, jnp.zeros((4, C), F32)], axis=0
    )
    part[0, KC : KC + 8] = small
    part[1, KC : KC + 8] = small

    core_copy = remote(part.at[1 - core], core_in, bs.at[0], br.at[0], member(z * 2 + 1 - core))
    core_copy.start()

    def out_copy(b):
        j = (b - m + M) % M
        return remote(ov.at[rows(b * R, R)], out_ref.at[own], os_.at[j], or_.at[j], member(b))

    own_out = pltpu.make_async_copy(ov.at[own], out_ref.at[own], os_.at[0])

    def send_out(b):
        start_if(b == m, own_out)
        start_if(b != m, out_copy(b))

    def grad_input(i, _):
        at = i * T
        recv_if((i == NT - 1) & (g < G - 1), g1_halo)
        mine = rows(at, T)
        total = (
            gh[mine].astype(F32)
            + dot(g1e[mine], w1t[0])
            + dot(g1e[rows(at + R, T)], w1t[1])
            + dot(g1e[rows(at + 2 * R, T)], w1t[2])
        )
        ov[mine] = total.astype(BF16)
        send_out(2 * i)
        send_out(2 * i + 1)
        return 0

    lax.fori_loop(0, NT, grad_input, 0)

    core_copy.wait()
    tail = part[core, KC : KC + 8] + core_in[KC : KC + 8]

    def fold(j, _):
        at = pl.ds(pl.multiple_of(j * SH, 8), SH)
        shard[j, 0:SH] = part[core, at] + core_in[at]
        shard[j, SH : SH + 8] = tail
        return 0

    lax.fori_loop(0, G, fold, 0)

    def sum_copy(j):
        p = (g + j) % G
        return remote(shard.at[p], r1.at[g], gs.at[j], gr.at[j], group(p))

    for j in range(1, G):
        sum_copy(j).start()
    r1[g] = shard[g]
    for j in range(1, G):
        sum_copy(j).wait()
    total = r1[0]
    for j in range(1, G):
        total = total + r1[j]

    def user_copy(j):
        return remote(r2.at[u], r2.at[u], us.at[j], ur.at[j], user((u + j) % U))

    r2[u] = total
    for j in range(1, U):
        user_copy(j).start()
    for j in range(1, U):
        user_copy(j).wait()
    total = r2[0]
    for j in range(1, U):
        total = total + r2[j]

    def z_copy(j):
        return remote(r3.at[z], r3.at[z], zs.at[j], zr.at[j], member((m + 2 * j) % M))

    r3[z] = total
    for j in range(1, M // 2):
        z_copy(j).start()
    for j in range(1, M // 2):
        z_copy(j).wait()
    total = r3[0]
    for j in range(1, M // 2):
        total = total + r3[j]
    total = total * scale
    final[...] = total[0:SH]
    for k, ref in enumerate((dg1, db1, dg2, db2)):
        ref[...] = total[SH + k : SH + k + 1]

    place = pl.ds(pl.multiple_of(core * KC + g * SH, 8), SH)

    def gather_copy(j):
        return remote(final, dw_ref.at[place], as_.at[j], ar.at[j], group((g + j) % G))

    own_sum = pltpu.make_async_copy(final, dw_ref.at[place], as_.at[0])
    own_sum.start()
    for j in range(1, G):
        gather_copy(j).start()
    own_sum.wait()
    for j in range(1, G):
        gather_copy(j).wait()
    layer = pl.ds(pl.multiple_of(core * KC, 8), KC)
    last_copy = remote(dw_ref.at[layer], dw_ref.at[layer], bs.at[1], br.at[1], member(z * 2 + 1 - core))
    last_copy.start()

    own_out.wait()
    for j in range(1, M):
        out_copy((m + j) % M).wait()
    send_done_if(g < G - 1, x_halo)
    send_done_if(g < G - 1, h_halo)
    send_done_if(g > 0, g2_halo)
    send_done_if(g > 0, g1_halo)
    last_copy.wait()


def shards(M, G, U, *args):
    inputs, first, gain1, bias1, second, gain2, bias2, cotangent = args
    _, length, C = inputs.shape
    R = length // M
    KC = 3 * C
    SH = KC // G
    N = length
    scale = float((length * M * G * U) ** -0.5)
    vmem, anyw = pl.BlockSpec(memory_space=pltpu.VMEM), pl.BlockSpec(memory_space=pl.ANY)
    vec = jax.ShapeDtypeStruct((1, C), F32)
    dma = pltpu.SemaphoreType.DMA
    out = pl.pallas_call(
        functools.partial(kernel, M, G, U, R, scale),
        out_shape=(
            jax.ShapeDtypeStruct((N, C), BF16),
            jax.ShapeDtypeStruct((2 * KC, C), F32),
            vec, vec, vec, vec,
        ),
        in_specs=[anyw] * 4 + [vmem] * 4,
        out_specs=(anyw, anyw, vmem, vmem, vmem, vmem),
        scratch_shapes=[
            pltpu.VMEM(((M + 2) * R, C), BF16),
            pltpu.VMEM((N, C), BF16),
            pltpu.VMEM(((M + 4) * R, C), BF16),
            pltpu.VMEM(((M + 4) * R, C), BF16),
            pltpu.VMEM(((M + 2) * R, C), BF16),
            pltpu.VMEM((C, (M + 2) * R), BF16),
            pltpu.VMEM((C, (M + 4) * R), BF16),
            *[pltpu.VMEM((3, C, C), BF16)] * 4,
            *[pltpu.VMEM((N, C), F32), pltpu.VMEM((N, 128), F32), pltpu.VMEM((N, C), F32)] * 2,
            *[pltpu.VMEM((N, C), BF16)] * 2,
            pltpu.VMEM((2, KC + 8, C), F32),
            pltpu.VMEM((KC + 8, C), F32),
            pltpu.VMEM((G, SH + 8, C), F32),
            pltpu.VMEM((G, SH + 8, C), F32),
            pltpu.VMEM((U, SH + 8, C), F32),
            pltpu.VMEM((M // 2, SH + 8, C), F32),
            pltpu.VMEM((SH, C), F32),
            dma((4,)),
            dma((M,)), dma((M,)),
            dma((M,)), dma((M,)),
            dma((M,)), dma((M,)),
            dma((4,)), dma((4,)),
            dma((1,)), dma((1,)),
            dma((G,)), dma((G,)),
            dma((U,)), dma((U,)),
            dma((M // 2,)), dma((M // 2,)),
            dma((G,)), dma((G,)),
            dma((2,)), dma((2,)),
        ],
        compiler_params=pltpu.CompilerParams(
            collective_id=0, has_side_effects=True, vmem_limit_bytes=40 * 2**20
        ),
    )(
        inputs.reshape(N, C), cotangent.reshape(N, C), first, second,
        *[v.reshape(1, C) for v in (gain1, bias1, gain2, bias2)],
    )
    grad, dw, dg1, db1, dg2, db2 = out
    dw = dw.reshape(2, 3, C, C)
    flat = [v.reshape(C) for v in (dg1, db1, dg2, db2)]
    return (grad.reshape(inputs.shape), dw[0], flat[0], flat[1], dw[1], flat[2], flat[3])


def solution(mesh):
    seq, users = mesh.shape["seq"], mesh.shape["user"]
    M = min(GROUP, seq)
    placed = (P("user", "seq", None), P(), P(), P(), P(), P(), P(), P("user", "seq", None))
    return jax.shard_map(
        functools.partial(shards, M, seq // M, users),
        mesh=mesh,
        in_specs=placed,
        out_specs=(P("user", "seq", None), P(), P(), P(), P(), P(), P()),
        check_vma=False,
    )
```

time: 917 us -> 136 us (0.15)
  waiting for transfers between devices: 563 us -> 0 us
  blocking collectives: 230 us -> 0 us
  Pallas kernels: 0 us -> 123 us
  starting transfers between devices: 81.5 us -> 0 us
  between operations: 14.5 us -> 0.66 us
  matrix products: 10.2 us -> 0 us
    psum x1 -> x0, waiting for transfers between devices: 460 us -> none  [shards(): lax.psum((weight_total_first, gain_total_first, bias_total_first, weight_...]
    psum x1 -> x0, blocking collectives: 230 us -> none  [shards(): lax.psum((weight_total_first, gain_total_first, bias_total_first, weight_...]
    pallas_call x0 -> x1, Pallas kernels: none -> 123 us  [shards(): pl.pallas_call(functools.partial(kernel, M, G, U, R, scale), out_shape=(j...]
    ppermute x8 -> x0, waiting for transfers between devices: 103 us -> none  [passed_along(): return lax.ppermute(shard, axis, pairs)]
    ppermute x8 -> x0, starting transfers between devices: 81.5 us -> none  [passed_along(): return lax.ppermute(shard, axis, pairs)]
    dot_general x18 -> x0, matrix products: 10.2 us -> none  [the longest x6 3.16 us: residual_layer_backward(): lax.dot_general(moved_all[offset], weight[offset], (((1,), (1,)), ((), ()...]
  transfers between devices with their start and end apart: 9 -> 0, of which waited for: 5 -> 0; matrix products, arithmetic and copies ran while one was open for 2% -> 0% of each run, Pallas kernels for 0% -> 0%
where the time goes in v1:
time: 136 us; the launch traced here: 134 us
  Pallas kernels  123 us (90%)
  local copies, waits for them, and re-layouts  11.1 us (8%)
    pallas_call x1, Pallas kernels, shards(): pl.pallas_call(functools.partial(kernel, M, G, U, R, scale), out_shape=(j...  123 us
    unnamed x21, local copies, waits for them, and re-layouts  9.82 us

profile of v1, /device:TPU:1, one launch (start us, length us, event | category | flops | bytes accessed | tf_op | source)
XLA Modules:
  0.0 134.4 jit_solution(9067979666116809556)
XLA Ops:
  0.6 0.0 copy-start
  0.6 1.0 copy-done
  1.7 0.0 copy-start.1
  1.7 1.0 copy-done.1
  2.7 0.0 copy-start.2
  2.7 1.0 copy-done.2
  3.7 0.0 copy-start.3
  3.7 1.0 copy-done.3
  4.7 0.0 copy-start.4
  4.7 0.7 copy-done.4
  5.4 0.0 copy-start.5
  5.4 0.7 copy-done.5
  6.1 0.0 copy-start.6
  6.1 0.7 copy-done.6
  6.8 0.0 copy-start.7
  6.8 0.7 copy-done.7
  7.4 122.7 %shard_map.135 = (bf16[1024,256]{1,0:T(8,128)(2,1)S(1)}, f32[1536,256]{1,0:T(8,128)S(1)}, f32[1,256]{1,0:T(1,128)S(1)}, f32[1,256]{1,0:T(1,128)S(1)}, f32[1,256]{1,0:T(1,128)S(1)}, /*index=5*/f32[1,256]{1,0:T(1,128)S(1)}) custom-call(bf16[1024,256]{1,0:T(8,128)(2,1)S(1)} %bitcast.13, bf16[1024,256]{1,0:T(8,128)(2,1)S(1)} %bitcast.14, ...), custom_call_target="tpu_custom_call" | custom-call | tf_op jit(solution)/shard_map/pallas_call | solution.py:366
  130.1 1.2 fusion
  131.3 0.8 copy.20
  132.1 0.6 copy.21
  132.7 0.6 copy.22
  133.3 0.6 copy.23
  133.8 0.6 copy.24
Async XLA Ops:
  0.6 1.0 copy-start
  1.7 1.0 copy-start.1
  2.7 1.0 copy-start.2
  3.7 1.0 copy-start.3
  4.7 0.7 copy-start.4
  5.4 0.7 copy-start.5
  6.1 0.7 copy-start.6
  6.8 0.7 copy-start.7

commit v2 on v0

v2 whole, which is shorter than its diff:
```python
import functools

import jax
import jax.numpy as jnp
from jax import lax
from jax.experimental import pallas as pl
from jax.experimental.pallas import tpu as pltpu
from jax.sharding import PartitionSpec as P

EPSILON = 1e-05
GROUP = 8
MESH = pl.DeviceIdType.MESH
F32 = jnp.float32
BF16 = jnp.bfloat16


def dot(a, b):
    return jnp.dot(a, b, preferred_element_type=F32)


def mean_c(values):
    return jnp.mean(values, axis=-1, keepdims=True)


PAIRS = 19


def kernel(
    M, G, U, R, QS, scale,
    x_ref, ct_ref, w1_ref, w2_ref, gain1_ref, bias1_ref, gain2_ref, bias2_ref,
    out_ref, dw_ref, small_ref,
    *scratch,
):
    pairs = [scratch[2 * k : 2 * k + 2] for k in range(PAIRS)]
    (xe, cte, he, g2e, g1e, xt0, xt1, xt2, ht0, ht1, ht2, n1, i1, s1, n2, i2, s2, gh, ov) = pairs
    xt, ht = (xt0, xt1, xt2), (ht0, ht1, ht2)
    (
        w1, w2, w1t, w2t, vecs,
        part, partb, small, small_all, core_in, shard, r1, piece, r2, r4, final,
        loc_sem, xs, xr, cs, cr, os_, or_, hs, hr, gs, gr, us, ur, zs, zr, as_, ar, bs, br,
    ) = scratch[2 * PAIRS :]
    C = x_ref.shape[1]
    NT = M // 4
    KC = 3 * C
    SR = 2 * KC // G
    PR = SR // U
    s, u = lax.axis_index("seq"), lax.axis_index("user")
    g, m = s // M, s % M
    core = m % 2
    z = m // 2

    def member(p):
        return {"seq": g * M + p, "user": u}

    def group(p):
        return {"seq": p * M + m, "user": u}

    def user(p):
        return {"seq": s, "user": p}

    H = M // 2
    Z = U * H
    column = u * H + z

    def on_z(p):
        return {"seq": g * M + 2 * (p % H) + core, "user": p // H}

    def remote(src, dst, ss, rs, device):
        return pltpu.make_async_remote_copy(
            src_ref=src, dst_ref=dst, send_sem=ss, recv_sem=rs, device_id=device, device_id_type=MESH
        )

    def rows(start, size):
        return pl.ds(pl.multiple_of(start, 16), size)

    barrier = pltpu.get_barrier_semaphore()
    far = [M // 2, M // 2 + 1]
    order = far + [j for j in range(M - 1, 0, -1) if j not in far]
    for j in order:
        pl.semaphore_signal(barrier, inc=1, device_id=member((m + j) % M), device_id_type=MESH)
    for j in range(1, G):
        pl.semaphore_signal(barrier, inc=1, device_id=group((g + j) % G), device_id_type=MESH)
    for j in range(1, Z):
        p = (column + j) % Z
        pl.when(p // H != u)(
            functools.partial(pl.semaphore_signal, barrier, inc=1, device_id=on_z(p), device_id_type=MESH)
        )

    def part_rows(p, a):
        return rows(p * R + (0, QS[0])[a], QS[a])

    local = [
        pltpu.make_async_copy(w1_ref, w1, loc_sem.at[0]),
        pltpu.make_async_copy(w2_ref, w2, loc_sem.at[1]),
    ]
    for k, ref in enumerate((gain1_ref, bias1_ref, gain2_ref, bias2_ref)):
        local.append(pltpu.make_async_copy(ref, vecs.at[k], loc_sem.at[2 + k]))
    for a in range(2):
        local.append(
            pltpu.make_async_copy(x_ref.at[part_rows(m, a)], xe[a].at[rows((2 + m) * QS[a], QS[a])], loc_sem.at[6 + a])
        )
        local.append(
            pltpu.make_async_copy(ct_ref.at[part_rows(m, a)], cte[a].at[rows(m * QS[a], QS[a])], loc_sem.at[8 + a])
        )
    for copy in local:
        copy.start()

    def x_copy(a, j):
        p = (m + j) % M
        return remote(x_ref.at[part_rows(p, a)], xe[a].at[rows((2 + m) * QS[a], QS[a])], xs.at[a, j], xr.at[a, j], member(p))

    def ct_copy(a, j):
        p = (m + j) % M
        return remote(ct_ref.at[part_rows(p, a)], cte[a].at[rows(m * QS[a], QS[a])], cs.at[a, j], cr.at[a, j], member(p))

    pl.semaphore_wait(barrier, M + G - 2 + Z - H)
    for copy in (x_copy, ct_copy):
        for a in range(2):
            for j in order:
                copy(a, j).start()

    def clear(buf, start, n):
        for a in range(2):
            buf[a][start * QS[a] : (start + n) * QS[a]] = jnp.zeros((n * QS[a], C), BF16)

    @pl.when(g == 0)
    def _():
        clear(xe, 0, 2)
        clear(he, 0, 4)

    @pl.when(g == G - 1)
    def _():
        clear(g2e, M, 4)
        clear(g1e, M, 2)

    later, earlier = group((g + 1) % G), group((g + G - 1) % G)

    def halo(buf, a, k, forward):
        n, Q = (4 if k in (1, 2) else 2), QS[a]
        head, tail = buf[a].at[0 : n * Q], buf[a].at[M * Q : (M + n) * Q]
        if forward:
            return remote(tail, head, hs.at[a, k], hr.at[a, k], later)
        return remote(head, tail, hs.at[a, k], hr.at[a, k], earlier)

    x_halo = [halo(xe, a, 0, True) for a in range(2)]
    h_halo = [halo(he, a, 1, True) for a in range(2)]
    g2_halo = [halo(g2e, a, 2, False) for a in range(2)]
    g1_halo = [halo(g1e, a, 3, False) for a in range(2)]
    not_first, not_last = g > 0, g < G - 1

    def start_if(cond, copy):
        pl.when(cond)(copy.start)

    def recv_if(cond, copy):
        pl.when(cond)(copy.wait_recv)

    for copy in local:
        copy.wait()
    for k in range(3):
        w1t[k] = w1[k].T
        w2t[k] = w2[k].T
    ga1, be1, ga2, be2 = vecs[0], vecs[1], vecs[2], vecs[3]

    def normalize(pre, gain, bias, a, mine, normed_ref, inverse_ref, slope_ref):
        away = pre - mean_c(pre)
        inverse = lax.rsqrt(mean_c(away * away) + EPSILON)
        normed = away * inverse
        active = normed * gain + bias
        sigma = 0.5 * jnp.tanh(0.5 * active) + 0.5
        normed_ref[a][mine] = normed
        inverse_ref[a][mine] = jnp.broadcast_to(inverse, (inverse.shape[0], 128))
        slope_ref[a][mine] = sigma * (1.0 + active * (1.0 - sigma))
        return active * sigma

    def tile(a, i, blocks=0):
        return pl.ds((4 * i + blocks) * QS[a], 4 * QS[a])

    def layer_one(a, i):
        here = xe[a][tile(a, i, 2)]
        pre = dot(here, w1[0]) + dot(xe[a][tile(a, i, 1)], w1[1]) + dot(xe[a][tile(a, i)], w1[2])
        gated = normalize(pre, ga1, be1, a, tile(a, i), n1, i1, s1)
        he[a][tile(a, i, 4)] = (here.astype(F32) + gated).astype(BF16)

    def layer_two(a, i):
        pre = dot(he[a][tile(a, i, 4)], w2[0]) + dot(he[a][tile(a, i, 2)], w2[1]) + dot(he[a][tile(a, i)], w2[2])
        normalize(pre, ga2, be2, a, tile(a, i), n2, i2, s2)

    for a in range(2):
        for j in range(1, M):
            x_copy(a, j).wait()
        start_if(not_last, x_halo[a])
        for i in range(NT - 1, -1, -1):
            if i == 0:
                recv_if(not_first, x_halo[a])
            layer_one(a, i)
            if i == NT - 1:
                start_if(not_last, h_halo[a])
    for a in range(2):
        for i in range(NT - 1, -1, -1):
            if i == 0:
                recv_if(not_first, h_halo[a])
            layer_two(a, i)
    for a in range(2):
        for k in range(3):
            ht[k][a][...] = he[a][pl.ds((4 - 2 * k) * QS[a], M * QS[a])].T
            xt[k][a][...] = xe[a][pl.ds((2 - k) * QS[a], M * QS[a])].T

    def norm_backward(grad, slope, normed, inverse, gain):
        g_act = grad * slope
        weighted = g_act * normed
        sums = (jnp.sum(weighted, axis=0, keepdims=True), jnp.sum(g_act, axis=0, keepdims=True))
        g_norm = g_act * gain
        g_pre = inverse * (g_norm - mean_c(g_norm) - normed * mean_c(weighted * gain))
        return g_pre.astype(BF16), sums

    def back_two(a, i):
        mine = tile(a, i)
        g_pre, sums = norm_backward(cte[a][mine].astype(F32), s2[a][mine], n2[a][mine], i2[a][mine, 0:1], ga2)
        g2e[a][mine] = g_pre
        return sums

    def back_one(a, i):
        mine = tile(a, i)
        total = (
            cte[a][mine].astype(F32)
            + dot(g2e[a][mine], w2t[0])
            + dot(g2e[a][tile(a, i, 2)], w2t[1])
            + dot(g2e[a][tile(a, i, 4)], w2t[2])
        )
        g_hidden = total.astype(BF16)
        gh[a][mine] = g_hidden
        g_pre, sums = norm_backward(g_hidden.astype(F32), s1[a][mine], n1[a][mine], i1[a][mine, 0:1], ga1)
        g1e[a][mine] = g_pre
        return sums

    def grad_input(a, i):
        mine = tile(a, i)
        total = (
            gh[a][mine].astype(F32)
            + dot(g1e[a][mine], w1t[0])
            + dot(g1e[a][tile(a, i, 1)], w1t[1])
            + dot(g1e[a][tile(a, i, 2)], w1t[2])
        )
        ov[a][mine] = total.astype(BF16)

    def weights(l, a):
        grads = (g1e, g2e)[l][a][0 : M * QS[a]]
        for k in range(3):
            at = pl.ds(k * C, C)
            total = dot((xt, ht)[l][k][a][...], grads)
            if a == 0:
                part[l, at] = total
            else:
                total = part[l, at] + total
                part[l, at] = total
                partb[l, at] = total.astype(BF16)

    def add(sums, more):
        return more if sums is None else (sums[0] + more[0], sums[1] + more[1])

    def out_copy(a, j):
        b = (m + j) % M
        return remote(ov[a].at[rows(b * QS[a], QS[a])], out_ref.at[part_rows(m, a)], os_.at[a, j], or_.at[a, j], member(b))

    def own_out(a):
        return pltpu.make_async_copy(ov[a].at[rows(m * QS[a], QS[a])], out_ref.at[part_rows(m, a)], os_.at[a, 0])

    def send_out(a):
        for j in order:
            out_copy(a, j).start()
        own_out(a).start()

    other = member(z * 2 + 1 - core)
    core_copy = remote(partb.at[1 - core], core_in, bs.at[0], br.at[0], other)

    def shard_copy(j):
        return remote(shard.at[(g + j) % G], r1.at[g], gs.at[0], gr.at[0], group((g + j) % G))

    all_shards = remote(r1.at[0 : G - 1], r1.at[0 : G - 1], gs.at[0], gr.at[0], other)

    def piece_copy(j):
        p = (column + j) % Z
        return remote(piece.at[p // H], r2.at[column], zs.at[0], zr.at[0], on_z(p))

    all_pieces = remote(r2.at[0 : Z - 1], r2.at[0 : Z - 1], zs.at[0], zr.at[0], other)

    def back_copy(j):
        return remote(r4.at[u], r4.at[u], us.at[j], ur.at[j], user((u + j) % U))

    place = dw_ref.at[rows(core * KC + (g // 2) * SR, SR), pl.ds(pl.multiple_of((g % 2) * 128, 128), 128)]

    def gather_copy(j):
        return remote(final, place, as_.at[0], ar.at[0], group((g + j) % G))

    all_gathered = remote(r1.at[0 : G - 1, 0:SR], r1.at[0 : G - 1, 0:SR], as_.at[0], ar.at[0], other)
    own_gather = pltpu.make_async_copy(final, place, bs.at[3])
    layer = dw_ref.at[rows(core * KC, KC)]
    last_copy = remote(layer, layer, bs.at[1], br.at[1], other)
    small_copy = remote(small_all.at[core], small_all.at[core], bs.at[2], br.at[2], other)

    def split(value):
        high = value.astype(BF16)
        return jnp.concatenate([high, (value - high.astype(F32)).astype(BF16)], axis=0)

    def joined(total):
        half = total.shape[0] // 2
        return total[:half] + total[half:]

    def pack_small(l, sums):
        value = jnp.concatenate(
            [v[:, at : at + 128] for v in sums for at in (0, 128)] + [jnp.zeros((4, 128), F32)], axis=0
        )
        small[l] = value
        partb[l, KC : KC + 16, 0:128] = split(value)

    def fold():
        core_copy.wait_recv()
        both = split(small[core] + joined(core_in[KC : KC + 16, 0:128].astype(F32)))
        for j in range(G):
            at, lanes = slice((j // 2) * SR, (j // 2 + 1) * SR), slice((j % 2) * 128, (j % 2 + 1) * 128)
            total = part[core, at, lanes] + core_in[at, lanes].astype(F32)
            shard[j, 0:SR] = total.astype(BF16)
            shard[j, SR : SR + 16] = both
        for j in range(1, G):
            shard_copy(j).start()
        r1[g] = shard[g]

    def added(ref, n):
        total = ref[0].astype(F32)
        for j in range(1, n):
            total = total + ref[j].astype(F32)
        return total

    def packed(total, value):
        high = value.astype(BF16).astype(F32)
        return jnp.concatenate([total, high, value - high], axis=0).astype(BF16)

    def over_z():
        all_shards.wait_recv()
        total = added(r1, G)
        value = joined(total[SR : SR + 16])[0:4]
        for j in range(U):
            piece[j] = packed(total[j * PR : (j + 1) * PR], value)
        for j in range(1, Z):
            piece_copy(j).start()
        r2[column] = piece[u]

    def back_to_users():
        all_pieces.wait_recv()
        total = added(r2, Z) * scale
        r4[u] = total.astype(BF16)
        for j in range(1, U):
            back_copy(j).start()
        small_all[core] = joined(total[PR : PR + 8])
        small_copy.start()

    def gather():
        for j in range(1, U):
            back_copy(j).wait_recv()
        final[...] = jnp.concatenate([r4[j].astype(F32)[0:PR] for j in range(U)], axis=0).astype(BF16)
        for j in range(1, G):
            gather_copy(j).start()
        own_gather.start()

    def last():
        own_gather.wait()
        all_gathered.wait_recv()
        last_copy.start()

    def sent():
        core_copy.wait_send()
        all_shards.wait_send()
        all_pieces.wait_send()
        for j in range(1, U):
            back_copy(j).wait_send()
        all_gathered.wait_send()

    sums_one = sums_two = None
    for a in range(2):
        for j in range(1, M):
            ct_copy(a, j).wait()
        for i in range(NT):
            sums_two = add(sums_two, back_two(a, i))
            if i == 0:
                start_if(not_first, g2_halo[a])
        if a == 1:
            pack_small(1, sums_two)
        weights(1, a)
        if a == 1:
            start_if(core == 0, core_copy)
        for i in range(NT):
            if i == NT - 1:
                if a == 1:
                    recv_if(not_last, g1_halo[0])
                    for k in range(NT):
                        grad_input(0, k)
                    send_out(0)
                    pl.when(core == 1)(fold)
                recv_if(not_last, g2_halo[a])
            sums_one = add(sums_one, back_one(a, i))
            if i == 0:
                start_if(not_first, g1_halo[a])
        if a == 1:
            pack_small(0, sums_one)
        weights(0, a)
    start_if(core == 1, core_copy)
    for i in range(NT - 1):
        grad_input(1, i)
    pl.when(core == 0)(fold)
    recv_if(not_last, g1_halo[1])
    grad_input(1, NT - 1)
    over_z()
    send_out(1)
    back_to_users()
    gather()
    last()
    small_copy.wait()
    for l in range(2):
        for k in range(2):
            small_ref[2 * l + k : 2 * l + k + 1] = jnp.concatenate(
                [small_all[l, 2 * k : 2 * k + 1], small_all[l, 2 * k + 1 : 2 * k + 2]], axis=1
            )

    for a in range(2):
        own_out(a).wait()
        for j in range(1, M):
            out_copy(a, j).wait()
        pl.when(not_last)(x_halo[a].wait_send)
        pl.when(not_last)(h_halo[a].wait_send)
        pl.when(not_first)(g2_halo[a].wait_send)
        pl.when(not_first)(g1_halo[a].wait_send)
    sent()
    last_copy.wait()


def shards(M, G, U, *args):
    inputs, first, gain1, bias1, second, gain2, bias2, cotangent = args
    _, N, C = inputs.shape
    R = N // M
    QS = (R - R // 4, R // 4)
    KC = 3 * C
    SR = 2 * KC // G
    PR = SR // U
    scale = float((N * M * G * U) ** -0.5)
    vmem, anyw = pl.BlockSpec(memory_space=pltpu.VMEM), pl.BlockSpec(memory_space=pl.ANY)
    dma = pltpu.SemaphoreType.DMA
    V = pltpu.VMEM

    def both(shape_of):
        return [shape_of(q) for q in QS]

    out = pl.pallas_call(
        functools.partial(kernel, M, G, U, R, QS, scale),
        out_shape=(
            jax.ShapeDtypeStruct((N, C), BF16),
            jax.ShapeDtypeStruct((2 * KC, C), BF16),
            jax.ShapeDtypeStruct((8, C), F32),
        ),
        in_specs=[anyw] * 8,
        out_specs=(anyw, anyw, vmem),
        scratch_shapes=[
            *both(lambda q: V(((M + 2) * q, C), BF16)),
            *both(lambda q: V((M * q, C), BF16)),
            *both(lambda q: V(((M + 4) * q, C), BF16)),
            *both(lambda q: V(((M + 4) * q, C), BF16)),
            *both(lambda q: V(((M + 2) * q, C), BF16)),
            *both(lambda q: V((C, M * q), BF16)) * 6,
            *(
                both(lambda q: V((M * q, C), F32))
                + both(lambda q: V((M * q, 128), F32))
                + both(lambda q: V((M * q, C), F32))
            )
            * 2,
            *both(lambda q: V((M * q, C), BF16)) * 2,
            *[V((3, C, C), BF16)] * 4,
            V((4, 1, C), F32),
            V((2, KC, C), F32),
            V((2, KC + 16, C), BF16),
            V((2, 8, 128), F32),
            V((2, 4, 128), F32),
            V((KC + 16, C), BF16),
            V((G, SR + 16, 128), BF16),
            V((G, SR + 16, 128), BF16),
            V((U, PR + 8, 128), BF16),
            V((U * M // 2, PR + 8, 128), BF16),
            V((U, PR + 8, 128), BF16),
            V((SR, 128), BF16),
            dma((10,)),
            dma((2, M)), dma((2, M)),
            dma((2, M)), dma((2, M)),
            dma((2, M)), dma((2, M)),
            dma((2, 4)), dma((2, 4)),
            dma((1,)), dma((1,)),
            dma((U,)), dma((U,)),
            dma((1,)), dma((1,)),
            dma((1,)), dma((1,)),
            dma((4,)), dma((3,)),
        ],
        compiler_params=pltpu.CompilerParams(
            collective_id=0, has_side_effects=True, vmem_limit_bytes=56 * 2**20
        ),
    )(
        inputs.reshape(N, C), cotangent.reshape(N, C), first, second,
        *[v.reshape(1, C) for v in (gain1, bias1, gain2, bias2)],
    )
    grad, dw, small = out
    dw = dw.reshape(2, 3, C, C).astype(F32)
    return (grad.reshape(inputs.shape), dw[0], small[0], small[1], dw[1], small[2], small[3])


def solution(mesh):
    seq, users = mesh.shape["seq"], mesh.shape["user"]
    M = min(GROUP, seq)
    placed = (P("user", "seq", None), P(), P(), P(), P(), P(), P(), P("user", "seq", None))
    return jax.shard_map(
        functools.partial(shards, M, seq // M, users),
        mesh=mesh,
        in_specs=placed,
        out_specs=(P("user", "seq", None), P(), P(), P(), P(), P(), P()),
        check_vma=False,
    )
```

time: 917 us -> 117 us (0.13)
  waiting for transfers between devices: 563 us -> 0 us
  blocking collectives: 230 us -> 0 us
  Pallas kernels: 0 us -> 112 us
  starting transfers between devices: 81.5 us -> 0 us
  between operations: 14.5 us -> 0.65 us
  matrix products: 10.2 us -> 0 us
    psum x1 -> x0, waiting for transfers between devices: 460 us -> none  [shards(): lax.psum((weight_total_first, gain_total_first, bias_total_first, weight_...]
    psum x1 -> x0, blocking collectives: 230 us -> none  [shards(): lax.psum((weight_total_first, gain_total_first, bias_total_first, weight_...]
    pallas_call x0 -> x1, Pallas kernels: none -> 112 us  [shards(): pl.pallas_call(functools.partial(kernel, M, G, U, R, QS, scale), out_shap...]
    ppermute x8 -> x0, waiting for transfers between devices: 103 us -> none  [passed_along(): return lax.ppermute(shard, axis, pairs)]
    ppermute x8 -> x0, starting transfers between devices: 81.5 us -> none  [passed_along(): return lax.ppermute(shard, axis, pairs)]
    dot_general x18 -> x0, matrix products: 10.2 us -> none  [the longest x6 3.16 us: residual_layer_backward(): lax.dot_general(moved_all[offset], weight[offset], (((1,), (1,)), ((), ()...]
  transfers between devices with their start and end apart: 9 -> 0, of which waited for: 5 -> 0; matrix products, arithmetic and copies ran while one was open for 2% -> 0% of each run, Pallas kernels for 0% -> 0%
where the time goes in v2:
time: 117 us
  Pallas kernels  112 us (96%)
  local copies, waits for them, and re-layouts  4.65 us (4%)
    pallas_call x1, Pallas kernels, shards(): pl.pallas_call(functools.partial(kernel, M, G, U, R, QS, scale), out_shap...  112 us
    slice x1, local copies, waits for them, and re-layouts, shards(): dw[1]  2.43 us

profile of v2, /device:TPU:1, one launch (start us, length us, event | category | flops | bytes accessed | tf_op | source)
XLA Modules:
  0.0 117.0 jit_solution(3484954123476821045)
XLA Ops:
  0.6 111.7 %shard_map.135 = (bf16[1024,256]{1,0:T(8,128)(2,1)}, bf16[1536,256]{1,0:T(8,128)(2,1)}, f32[8,256]{1,0:T(8,128)}) custom-call(bf16[1024,256]{1,0:T(8,128)(2,1)} %bitcast.15, bf16[1024,256]{1,0:T(8,128)(2,1)} %bitcast.16, bf16[3,256,256]{2,1,0:T(8,128)(2,1)} %w1_ref.1, bf16[3,256,256]{2,1,0:T(8,128)(2,1)} %w2_ref.1, f32[1,256]{1,0:T(1,128)} %bitcast.18, ...), custom_call_target="tpu_custom_call" | custom-call | tf_op jit(solution)/shard_map/pallas_call | solution.py:452
  112.4 1.4 %fusion.1 = (f32[1,256]{1,0:T(1,128)}, f32[1,256]{1,0:T(1,128)}, f32[1,256]{1,0:T(1,128)}, f32[1,256]{1,0:T(1,128)}) fusion(f32[8,256]{1,0:T(8,128)} %get-tuple-element.12), kind=kLoop, calls=%fused_computation.1 | loop fusion | bytes 8192 | tf_op jit(solution)/shard_map/slice | solution.py:508
  113.8 0.0 copy-start
  113.8 2.4 %fusion = (f32[768,256]{1,0:T(8,128)}, f32[768,256]{1,0:T(8,128)}) fusion(bf16[1536,256]{1,0:T(8,128)(2,1)} %get-tuple-element.11), kind=kLoop, calls=%fused_computation | loop fusion | bytes 3145728 | tf_op jit(solution)/shard_map/slice | solution.py:508
  116.2 0.0 copy-done
  116.2 0.8 copy.16
Async XLA Ops:
  113.8 2.4 %copy-start = (bf16[1024,256]{1,0:T(8,128)(2,1)S(1)}, bf16[1024,256]{1,0:T(8,128)(2,1)}, u32[]{:S(2)}) copy-start(bf16[1024,256]{1,0:T(8,128)(2,1)} %get-tuple-element.10) | copy-start | bytes 1572868

commit v3 on v2

--- a/solution.py
+++ b/solution.py
@@ -73,18 +73,22 @@
     def rows(start, size):
         return pl.ds(pl.multiple_of(start, 16), size)
 
+    g_order = sorted(range(1, G), key=lambda j: -(min(j % 4, 4 - j % 4) + min(j // 4, 4 - j // 4)))
+    z_order = sorted(range(1, Z), key=lambda j: -min(j % H, H - j % H))
+
     barrier = pltpu.get_barrier_semaphore()
     far = [M // 2, M // 2 + 1]
     order = far + [j for j in range(M - 1, 0, -1) if j not in far]
     for j in order:
         pl.semaphore_signal(barrier, inc=1, device_id=member((m + j) % M), device_id_type=MESH)
-    for j in range(1, G):
-        pl.semaphore_signal(barrier, inc=1, device_id=group((g + j) % G), device_id_type=MESH)
-    for j in range(1, Z):
+    for j in z_order:
         p = (column + j) % Z
         pl.when(p // H != u)(
             functools.partial(pl.semaphore_signal, barrier, inc=1, device_id=on_z(p), device_id_type=MESH)
         )
+
+    for j in g_order:
+        pl.semaphore_signal(barrier, inc=1, device_id=group((g + j) % G), device_id_type=MESH)
 
     def part_rows(p, a):
         return rows(p * R + (0, QS[0])[a], QS[a])
@@ -321,7 +325,7 @@
             total = part[core, at, lanes] + core_in[at, lanes].astype(F32)
             shard[j, 0:SR] = total.astype(BF16)
             shard[j, SR : SR + 16] = both
-        for j in range(1, G):
+        for j in g_order:
             shard_copy(j).start()
         r1[g] = shard[g]
 
@@ -341,7 +345,7 @@
         value = joined(total[SR : SR + 16])[0:4]
         for j in range(U):
             piece[j] = packed(total[j * PR : (j + 1) * PR], value)
-        for j in range(1, Z):
+        for j in z_order:
             piece_copy(j).start()
         r2[column] = piece[u]
 
@@ -358,7 +362,7 @@
         for j in range(1, U):
             back_copy(j).wait_recv()
         final[...] = jnp.concatenate([r4[j].astype(F32)[0:PR] for j in range(U)], axis=0).astype(BF16)
-        for j in range(1, G):
+        for j in g_order:
             gather_copy(j).start()
         own_gather.start()
 
@@ -395,7 +399,6 @@
                     for k in range(NT):
                         grad_input(0, k)
                     send_out(0)
-                    pl.when(core == 1)(fold)
                 recv_if(not_last, g2_halo[a])
             sums_one = add(sums_one, back_one(a, i))
             if i == 0:
@@ -406,7 +409,7 @@
     start_if(core == 1, core_copy)
     for i in range(NT - 1):
         grad_input(1, i)
-    pl.when(core == 0)(fold)
+    fold()
     recv_if(not_last, g1_halo[1])
     grad_input(1, NT - 1)
     over_z()

time: 117 us -> 116 us (level)
  no operation moved by 1% of the time
where the time goes in v3:
time: 116 us
  Pallas kernels  111 us (96%)
  local copies, waits for them, and re-layouts  4.65 us (4%)
    pallas_call x1, Pallas kernels, shards(): pl.pallas_call(functools.partial(kernel, M, G, U, R, QS, scale), out_shap...  111 us
    slice x1, local copies, waits for them, and re-layouts, shards(): dw[1]  2.43 us

profile of v3, /device:TPU:1, one launch (start us, length us, event | category | flops | bytes accessed | tf_op | source)
XLA Modules:
  0.0 116.3 jit_solution(7713157294586977970)
XLA Ops:
  0.6 111.0 %shard_map.135 = (bf16[1024,256]{1,0:T(8,128)(2,1)}, bf16[1536,256]{1,0:T(8,128)(2,1)}, f32[8,256]{1,0:T(8,128)}) custom-call(bf16[1024,256]{1,0:T(8,128)(2,1)} %bitcast.15, bf16[1024,256]{1,0:T(8,128)(2,1)} %bitcast.16, bf16[3,256,256]{2,1,0:T(8,128)(2,1)} %w1_ref.1, bf16[3,256,256]{2,1,0:T(8,128)(2,1)} %w2_ref.1, f32[1,256]{1,0:T(1,128)} %bitcast.18, ...), custom_call_target="tpu_custom_call" | custom-call | tf_op jit(solution)/shard_map/pallas_call | solution.py:455
  111.6 1.4 %fusion.1 = (f32[1,256]{1,0:T(1,128)}, f32[1,256]{1,0:T(1,128)}, f32[1,256]{1,0:T(1,128)}, f32[1,256]{1,0:T(1,128)}) fusion(f32[8,256]{1,0:T(8,128)} %get-tuple-element.12), kind=kLoop, calls=%fused_computation.1 | loop fusion | bytes 8192 | tf_op jit(solution)/shard_map/slice | solution.py:511
  113.0 0.0 copy-start
  113.0 2.4 %fusion = (f32[768,256]{1,0:T(8,128)}, f32[768,256]{1,0:T(8,128)}) fusion(bf16[1536,256]{1,0:T(8,128)(2,1)} %get-tuple-element.11), kind=kLoop, calls=%fused_computation | loop fusion | bytes 3145728 | tf_op jit(solution)/shard_map/slice | solution.py:511
  115.5 0.0 copy-done
  115.5 0.8 copy.16
Async XLA Ops:
  113.0 2.4 %copy-start = (bf16[1024,256]{1,0:T(8,128)(2,1)S(1)}, bf16[1024,256]{1,0:T(8,128)(2,1)}, u32[]{:S(2)}) copy-start(bf16[1024,256]{1,0:T(8,128)(2,1)} %get-tuple-element.10) | copy-start | bytes 1572868

commit v4 on v3

--- a/solution.py
+++ b/solution.py
@@ -413,8 +413,8 @@
     recv_if(not_last, g1_halo[1])
     grad_input(1, NT - 1)
     over_z()
+    back_to_users()
     send_out(1)
-    back_to_users()
     gather()
     last()
     small_copy.wait()

time: 116 us -> 114 us (0.983)
  Pallas kernels: 111 us -> 108 us
    pallas_call x1, Pallas kernels: 111 us -> 108 us  [shards(): pl.pallas_call(functools.partial(kernel, M, G, U, R, QS, scale), out_shap...]
where the time goes in v4:
time: 114 us; the launch traced here: 113 us
  Pallas kernels  108 us (95%)
  local copies, waits for them, and re-layouts  4.65 us (4%)
    pallas_call x1, Pallas kernels, shards(): pl.pallas_call(functools.partial(kernel, M, G, U, R, QS, scale), out_shap...  108 us
    slice x1, local copies, waits for them, and re-layouts, shards(): dw[1]  2.43 us

profile of v4, /device:TPU:1, one launch (start us, length us, event | category | flops | bytes accessed | tf_op | source)
XLA Modules:
  0.0 113.5 jit_solution(9025940656673761022)
XLA Ops:
  0.6 108.2 %shard_map.135 = (bf16[1024,256]{1,0:T(8,128)(2,1)}, bf16[1536,256]{1,0:T(8,128)(2,1)}, f32[8,256]{1,0:T(8,128)}) custom-call(bf16[1024,256]{1,0:T(8,128)(2,1)} %bitcast.15, bf16[1024,256]{1,0:T(8,128)(2,1)} %bitcast.16, bf16[3,256,256]{2,1,0:T(8,128)(2,1)} %w1_ref.1, bf16[3,256,256]{2,1,0:T(8,128)(2,1)} %w2_ref.1, f32[1,256]{1,0:T(1,128)} %bitcast.18, ...), custom_call_target="tpu_custom_call" | custom-call | tf_op jit(solution)/shard_map/pallas_call | solution.py:455
  108.8 1.4 %fusion.1 = (f32[1,256]{1,0:T(1,128)}, f32[1,256]{1,0:T(1,128)}, f32[1,256]{1,0:T(1,128)}, f32[1,256]{1,0:T(1,128)}) fusion(f32[8,256]{1,0:T(8,128)} %get-tuple-element.12), kind=kLoop, calls=%fused_computation.1 | loop fusion | bytes 8192 | tf_op jit(solution)/shard_map/slice | solution.py:511
  110.3 0.0 copy-start
  110.3 2.4 %fusion = (f32[768,256]{1,0:T(8,128)}, f32[768,256]{1,0:T(8,128)}) fusion(bf16[1536,256]{1,0:T(8,128)(2,1)} %get-tuple-element.11), kind=kLoop, calls=%fused_computation | loop fusion | bytes 3145728 | tf_op jit(solution)/shard_map/slice | solution.py:511
  112.7 0.0 copy-done
  112.7 0.8 copy.16
Async XLA Ops:
  110.3 2.4 %copy-start = (bf16[1024,256]{1,0:T(8,128)(2,1)S(1)}, bf16[1024,256]{1,0:T(8,128)(2,1)}, u32[]{:S(2)}) copy-start(bf16[1024,256]{1,0:T(8,128)(2,1)} %get-tuple-element.10) | copy-start | bytes 1572868
